TPU v7x, 32 devices: a whole 2x2x4 slice. The times are simulated.
32 devices in a mesh: dp: 32 (over z, y, x, core).
Axes of the slice: x: 2, y: 2, z: 4, core: 2. Of those that a mesh axis runs over, the one named last changes fastest.
Arguments:
- inputs: bfloat16 [31520, 384], P('dp'), may hold values from -6 to 6
- weights: bfloat16 [13824, 128], P('dp'), may hold values from -0.8164966 to 0.8164966
- vectors: float32 [36, 128], replicated, may hold values from -2 to 2
- cotangent: bfloat16 [31520, 384], P('dp'), may hold values from -6 to 6
- mom_weights: float32 [13824, 128], P('dp'), may hold values from -213.046474 to 213.046474
- mom_vectors: float32 [36, 128], replicated, may hold values from -355.07746 to 355.07746
Outputs:
- output: bfloat16 [31520, 384], P('dp')
- grad_inputs: float32 [31520, 384], P('dp')
- grad_weights: float32 [13824, 128], P('dp')
- grad_vectors: float32 [36, 128], replicated
- new_mom_weights: float32 [13824, 128], P('dp')
- new_mom_vectors: float32 [36, 128], replicated
- update_weights: float32 [13824, 128], P('dp')
- update_vectors: float32 [36, 128], replicated
All inputs are finite; a program needn't handle non-finite values.
Results may differ from a plain program's by a relative error of at most 0.012.
Values may be sent and summed in bfloat16 or wider, within the bound.
A program may use at most 128 MiB of HBM per device.

v0:
```python
import math
import jax
import jax.numpy as jnp
from jax import lax
from jax.sharding import PartitionSpec as P

D = 384
HEADS = 6
HD = 64
FF = 1536
SEQ = 197
HIGH = lax.Precision.HIGHEST
MOMENTUM = 0.95
MATRIX_RATE = 0.5
VECTOR_RATE = 0.2
NEWTON_COEFFS = (3.4445, -4.775, 2.0315)
NORM_EPS = 1e-06


def split_matrices(flat):
    flat_line = flat.reshape(-1)
    layout = ((D, 3 * D), (D, D), (D, FF), (FF, D))
    pieces = []
    offset = 0
    for dims_pair in layout:
        entries = dims_pair[0] * dims_pair[1]
        pieces.append(flat_line[offset : offset + entries].reshape(dims_pair))
        offset = offset + entries
    return pieces


def split_vectors(flat):
    flat_line = flat.reshape(-1)
    pieces = []
    offset = 0
    for length_one in (D, D, D, D, D, D, D, D, FF):
        pieces.append(flat_line[offset : offset + length_one])
        offset = offset + length_one
    return pieces


def layer_norm(value, norm_gain, norm_shift):
    center = jnp.mean(value, axis=-1, keepdims=True)
    deviation = value - center
    spread = jnp.mean(deviation * deviation, axis=-1, keepdims=True)
    return deviation * lax.rsqrt(spread + NORM_EPS) * norm_gain + norm_shift


def gelu_exact(value):
    return jax.nn.gelu(value, approximate=False)


def matmul(left, right):
    return jnp.dot(left, right, preferred_element_type=jnp.float32)


def outer_sum(left, right):
    return lax.dot_general(
        left, right, (((0,), (0,)), ((), ())), preferred_element_type=jnp.float32
    )


def times_transpose(left, right):
    return lax.dot_general(
        left, right, (((1,), (1,)), ((), ())), preferred_element_type=jnp.float32
    )


def column_sums(value):
    return jnp.sum(value.astype(jnp.float32), axis=0)


def orthogonalize(matrix):
    tall = matrix.shape[0] > matrix.shape[1]
    current = matrix.T if tall else matrix
    current = current / (jnp.sqrt(jnp.sum(current * current)) + 1e-07)
    first, second, third = NEWTON_COEFFS
    for repeat in range(5):
        square = jnp.dot(current, current.T, precision=HIGH)
        poly = second * square + third * jnp.dot(square, square, precision=HIGH)
        current = first * current + jnp.dot(poly, current, precision=HIGH)
    return current.T if tall else current


def blank_like(matrix):
    return jnp.zeros_like(matrix)


def on_device(inputs, weights, vectors, cotangent, mom_weights, mom_vectors):
    count = lax.axis_size("dp")
    device_index = lax.axis_index("dp")
    whole = lax.all_gather(weights, "dp", axis=0, tiled=True)
    w_qkv, w_out, w_up, w_down = split_matrices(whole)
    ln1_gain, ln1_shift, bias_q, bias_v, bias_out, ln2_gain, ln2_shift, bias_down, bias_up = (
        split_vectors(vectors)
    )
    rows = inputs.shape[0]
    images = rows // SEQ
    scale_qk = HD ** (-0.5)
    residual_in = inputs.astype(jnp.float32)
    normed, norm_pull = jax.vjp(layer_norm, residual_in, ln1_gain, ln1_shift)
    normed_low = normed.astype(jnp.bfloat16)
    bias_qkv = jnp.concatenate([bias_q, jnp.zeros_like(bias_q), bias_v])
    qkv = (
        (matmul(normed_low, w_qkv) + bias_qkv)
        .astype(jnp.bfloat16)
        .reshape(images, SEQ, 3, HEADS, HD)
    )
    queries = qkv[:, :, 0]
    key_rows = qkv[:, :, 1]
    values = qkv[:, :, 2]
    scores = (
        jnp.einsum("bqhd,bkhd->bhqk", queries, key_rows, preferred_element_type=jnp.float32)
        * scale_qk
    )
    row_max = jnp.max(scores, axis=-1, keepdims=True)
    log_total = row_max + jnp.log(jnp.sum(jnp.exp(scores - row_max), axis=-1, keepdims=True))
    probs_low = jnp.exp(scores - log_total).astype(jnp.bfloat16)
    attended = jnp.einsum("bhqk,bkhd->bqhd", probs_low, values, preferred_element_type=jnp.float32)
    attended = attended.reshape(rows, D).astype(jnp.bfloat16)
    middle = residual_in + matmul(attended, w_out) + bias_out
    normed_two, norm_pull_two = jax.vjp(layer_norm, middle, ln2_gain, ln2_shift)
    normed_two_low = normed_two.astype(jnp.bfloat16)
    hidden = matmul(normed_two_low, w_up) + bias_up
    unused_out, gelu_pull = jax.vjp(gelu_exact, hidden)
    active = gelu_exact(hidden).astype(jnp.bfloat16)
    result = middle + matmul(active, w_down) + bias_down
    output = result.astype(jnp.bfloat16)
    again = lax.all_gather(weights, "dp", axis=0, tiled=True)
    w_qkv, w_out, w_up, w_down = split_matrices(again)
    grad_down = outer_sum(active, cotangent)
    grad_bias_down = column_sums(cotangent)
    d_active = times_transpose(cotangent, w_down)
    d_hidden = gelu_pull(d_active)[0].astype(jnp.bfloat16)
    grad_up = outer_sum(normed_two_low, d_hidden)
    grad_bias_up = column_sums(d_hidden)
    d_normed_two = times_transpose(d_hidden, w_up)
    d_middle_norm, grad_ln2_gain, grad_ln2_shift = norm_pull_two(d_normed_two)
    d_middle = cotangent.astype(jnp.float32) + d_middle_norm
    d_branch = d_middle.astype(jnp.bfloat16)
    grad_out = outer_sum(attended, d_branch)
    grad_bias_out = column_sums(d_branch)
    d_attended = (
        times_transpose(d_branch, w_out).astype(jnp.bfloat16).reshape(images, SEQ, HEADS, HD)
    )
    scores_again = (
        jnp.einsum("bqhd,bkhd->bhqk", queries, key_rows, preferred_element_type=jnp.float32)
        * scale_qk
    )
    probs_full = jnp.exp(scores_again - log_total)
    probs_again = probs_full.astype(jnp.bfloat16)
    grad_values = jnp.einsum(
        "bhqk,bqhd->bkhd", probs_again, d_attended, preferred_element_type=jnp.float32
    )
    d_probs = jnp.einsum("bqhd,bkhd->bhqk", d_attended, values, preferred_element_type=jnp.float32)
    d_scores = probs_full * (d_probs - jnp.sum(d_probs * probs_full, axis=-1, keepdims=True))
    d_scores = d_scores.astype(jnp.bfloat16)
    grad_queries = (
        jnp.einsum("bhqk,bkhd->bqhd", d_scores, key_rows, preferred_element_type=jnp.float32)
        * scale_qk
    )
    grad_keys = (
        jnp.einsum("bhqk,bqhd->bkhd", d_scores, queries, preferred_element_type=jnp.float32)
        * scale_qk
    )
    d_qkv = (
        jnp.stack([grad_queries, grad_keys, grad_values], axis=2)
        .astype(jnp.bfloat16)
        .reshape(rows, 3 * D)
    )
    grad_qkv = outer_sum(normed_low, d_qkv)
    grad_bias_q = column_sums(d_qkv[:, :D])
    grad_bias_v = column_sums(d_qkv[:, 2 * D :])
    d_normed = times_transpose(d_qkv, w_qkv)
    d_input_norm, grad_ln1_gain, grad_ln1_shift = norm_pull(d_normed)
    grad_inputs = d_middle + d_input_norm
    local_grads = jnp.concatenate(
        [grad_qkv.reshape(-1), grad_out.reshape(-1), grad_up.reshape(-1), grad_down.reshape(-1)]
    )
    local_grads = local_grads.reshape(-1, 128)
    local_vector_grads = jnp.concatenate(
        [
            grad_ln1_gain,
            grad_ln1_shift,
            grad_bias_q,
            grad_bias_v,
            grad_bias_out,
            grad_ln2_gain,
            grad_ln2_shift,
            grad_bias_down,
            grad_bias_up,
        ]
    ).reshape(-1, 128)
    grad_vectors = lax.psum(local_vector_grads, "dp")
    grad_weights = lax.psum_scatter(local_grads, "dp", scatter_dimension=0, tiled=True)
    new_mom_weights = MOMENTUM * mom_weights + grad_weights
    gathered = lax.all_gather(new_mom_weights, "dp", axis=0, tiled=True)
    new_mom_vectors = MOMENTUM * mom_vectors + grad_vectors
    mom_matrices = split_matrices(gathered)
    owned_list = []
    for matrix_slot in range(4):
        owner_rank = 0
        computed = lax.cond(
            device_index == owner_rank, orthogonalize, blank_like, mom_matrices[matrix_slot]
        )
        owned_list.append(computed)
    owned_flat = jnp.concatenate([item.reshape(-1) for item in owned_list]).reshape(-1, 128)
    own_rows = lax.psum_scatter(owned_flat, "dp", scatter_dimension=0, tiled=True)
    update_weights = -MATRIX_RATE * own_rows
    total_tokens = rows * count
    update_vectors = -(VECTOR_RATE / math.sqrt(total_tokens)) * new_mom_vectors
    return (
        output,
        grad_inputs,
        grad_weights,
        grad_vectors,
        new_mom_weights,
        new_mom_vectors,
        update_weights,
        update_vectors,
    )


def solution(mesh):
    in_specs = (P("dp", None), P("dp", None), P(), P("dp", None), P("dp", None), P())
    out_specs = (
        P("dp", None),
        P("dp", None),
        P("dp", None),
        P(),
        P("dp", None),
        P(),
        P("dp", None),
        P(),
    )
    return jax.shard_map(
        on_device, mesh=mesh, in_specs=in_specs, out_specs=out_specs, check_vma=False
    )
```

profile of v0, /device:TPU:0, one launch (start us, length us, event | category | flops | bytes accessed | tf_op | source)
XLA Modules:
  0.0 743.2 jit_solution(9406631774744465408)
XLA Ops:
  14.8 58.9 %all-gather.3.cloned.1.call-done = bf16[13824,128]{1,0:T(8,128)(2,1)} async-done(((bf16[432,128]{1,0:T(8,128)(2,1)}), bf16[13824,128]{1,0:T(8,128)(2,1)}) %all-gather.3.cloned.1.call-update) | async-done | bytes 3538960 | tf_op jit(solution)/shard_map/all_gather | solution.py:92
  85.0 5.7 reshape.262
  90.7 5.8 fusion.79
  96.5 3.3 copy.51
  99.8 4.1 copy.50
  103.9 3.6 copy.52
  115.7 15.7 %multiply_convert_fusion.1 = (bf16[985,1536]{1,0:T(8,128)(2,1)}, f32[985,1536]{1,0:T(8,128)S(1)}, f32[985,1536]{1,0:T(8,128)S(1)}) fusion(f32[1536]{0:T(1024)S(1)} %copy-done.31, bf16[384,1536]{1,0:T(8,128)(2,1)S(1)} %copy-done.24, f32[985,384]{1,0:T(8,128)S(1)} %get-tuple-element.75, f32[384]{0:T(512)S(1)} %copy-done.36, f32[384]{0:T(512)S(1)} %get-tuple-element.66, ...), kind=kOutput, calls=%fused_computation.96 | convolution fusion | flops 1263699840 | bytes 17839304 | tf_op jit(solution)/shard_map/dot_general | solution.py:54
  131.5 4.0 convert_reduce_fusion
  146.1 3.8 copy.35
  149.9 5.4 convolution_bitcast_fusion
  164.0 3.3 fusion.102
  177.2 4.5 copy.40
  181.7 7.6 %convert_element_type.97 = bf16[985,1152]{0,1:T(8,128)(2,1)} reshape(bf16[5,197,3,6,64]{1,0,4,3,2:T(8,128)(2,1)} %copy.40) | data formatting | bytes 4538880 | tf_op jit(solution)/shard_map/convert_element_type | solution.py:168
  189.2 4.5 fusion.69
  196.2 8.8 %maximum_bitcast_fusion = f32[13824,128]{1,0:T(8,128)} fusion(f32[589824]{0:T(1024)S(1)} %reshape.258, f32[589824]{0:T(1024)} %reshape.257, f32[147456]{0:T(1024)} %reshape.256, f32[442368]{0:T(1024)} %reshape.255), kind=kLoop, calls=%fused_computation.87 | loop fusion | flops 5308416 | bytes 14155776 | tf_op jit(solution)/shard_map/reshape | solution.py:180
  205.1 118.2 %reduce-scatter.3.cloned.1.call-done = f32[432,128]{1,0:T(8,128)} async-done(((f32[13824,128]{1,0:T(8,128)}), f32[432,128]{1,0:T(8,128)}) %reduce-scatter.3.cloned.1.call-update) | async-done | bytes 221200 | tf_op jit(solution)/shard_map/reduce_scatter | solution.py:195
  325.0 73.9 %all-gather.5.cloned.1.call-done = f32[13824,128]{1,0:T(8,128)} async-done(((f32[432,128]{1,0:T(8,128)}), f32[13824,128]{1,0:T(8,128)}) %all-gather.5.cloned.1.call-update) | async-done | bytes 7077904 | tf_op jit(solution)/shard_map/all_gather | solution.py:197
  398.9 25.2 %conditional.5 = (f32[147456]{0:T(1024)S(1)}) conditional(s32[]{:T(128)} %convert_element_type.102, () %tuple.41, f32[13824,128]{1,0:T(8,128)} %all-gather.5.cloned.1.call-done), branch_computations={%region_25.0_spmd, %region_26.28_spmd} | conditional | flops 10196287488 | bytes 24772644 | solution.py:203
  424.9 50.1 %conditional.4 = (f32[442368]{0:T(1024)S(1)}) conditional(s32[]{:T(128)} %convert_element_type.102, () %tuple.40, f32[13824,128]{1,0:T(8,128)} %all-gather.5.cloned.1.call-done), branch_computations={%region_22.0_spmd, %region_23.25_spmd} | conditional | flops 23789666304 | bytes 50724900 | solution.py:203
  456.1 3.4 fusion.85
  468.6 4.5 convolution_add_fusion
  476.2 76.1 %conditional.7 = (f32[589824]{0:T(1024)S(1)}) conditional(s32[]{:T(128)} %convert_element_type.102, () %tuple.43, f32[13824,128]{1,0:T(8,128)} %all-gather.5.cloned.1.call-done), branch_computations={%region_31.32_spmd, %region_32.34_spmd} | conditional | flops 30598152192 | bytes 141557856 | solution.py:203
  479.8 3.4 broadcast_multiply_fusion
  490.5 3.9 fusion.97
  495.7 5.3 fusion.98
  503.0 9.1 %fusion.32 = f32[384,384]{1,0:T(8,128)S(1)} fusion(f32[384,1536]{1,0:T(8,128)} %fusion.98, f32[1536,384]{0,1:T(8,128)} %copy.25), kind=kOutput, calls=%fused_computation.85 | convolution fusion | flops 2719088640 | bytes 5308416 | tf_op jit(solution)/shard_map/cond/branch_1_fun/dot_general | solution.py:79
  513.4 4.3 multiply_add_fusion.2
  517.7 4.0 fusion.99
  523.0 4.3 fusion.100
  527.3 4.2 fusion.30
  532.8 4.0 fusion.29
  536.8 4.7 fusion.19
  542.8 4.9 convolution_add_fusion.15
  553.7 58.4 %conditional.6 = (f32[589824]{0:T(1024)}) conditional(s32[]{:T(128)} %convert_element_type.102, () %tuple.42, f32[13824,128]{1,0:T(8,128)} %all-gather.5.cloned.1.call-done), branch_computations={%region_28.0_spmd, %region_29.31_spmd} | conditional | flops 30586355712 | bytes 63701028 | solution.py:203
  562.9 4.0 fusion.92
  568.2 4.0 convolution_add_fusion.14
  572.2 4.5 fusion.93
  578.0 4.0 convolution_add_fusion.13
  582.0 4.0 fusion.94
  587.3 4.2 convolution_add_fusion.12
  591.5 4.0 fusion.95
  596.8 4.0 convolution_add_fusion.11
  600.8 4.2 fusion.96
  606.4 4.0 convolution_add_fusion.10
  612.2 7.3 maximum_bitcast_fusion.1
  627.8 37.0 %psum.7 = f32[36,128]{1,0:T(8,128)S(1)} all-reduce(f32[36,128]{1,0:T(8,128)S(1)} %bitcast.231), channel_id=1, replica_groups=mesh['dp'=32] {'dp'}, use_global_device_ids=true, to_apply=%region_21.0 | all-reduce | flops 4608 | bytes 36864 | tf_op jit(solution)/shard_map/psum | solution.py:194
  665.4 5.7 add_convert_fusion.1
  671.1 63.5 %reduce-scatter.5.cloned.1.call-done = f32[432,128]{1,0:T(8,128)} async-done(((f32[13824,128]{1,0:T(8,128)}), f32[432,128]{1,0:T(8,128)}) %reduce-scatter.5.cloned.1.call-update) | async-done | bytes 221200 | tf_op jit(solution)/shard_map/reduce_scatter | solution.py:208
  (210 shorter events, 177.3 us)
Async XLA Ops:
  7.2 66.5 %all-gather.3.cloned.1.call-start = ((), (), s32[]{:S(2)}) async-start(), calls=%async_computation.2 | async-start | bytes 3649536 | tf_op jit(solution)/shard_map/all_gather | solution.py:92
  7.9 315.4 %reduce-scatter.3.cloned.1.call-start = ((), (), s32[]{:S(2)}) async-start(), calls=%async_computation.3 | async-start | bytes 7299072 | tf_op jit(solution)/shard_map/reduce_scatter | solution.py:195
  12.9 0.6 copy-start.27
  73.7 1.3 slice-start.2
  78.7 3.6 copy-start.3
  78.7 3.6 copy-start.30
  78.7 3.6 copy-start.34
  99.8 7.6 %copy-start.10 = (bf16[5,197,1,6,64]{1,4,3,0,2:T(8,128)(2,1)}, bf16[5,197,1,6,64]{1,4,3,0,2:T(8,128)(2,1)S(1)}, u32[]{:S(2)}) copy-start(bf16[5,197,1,6,64]{1,4,3,0,2:T(8,128)(2,1)S(1)} %copy.51) | copy-start | bytes 2269444
  107.5 1.1 copy-start.12
  108.5 2.6 copy-start
  108.6 2.6 copy-start.14
  112.4 2.0 copy-start.32
  114.4 1.3 copy-start.24
  114.4 1.3 copy-start.31
  114.5 1.3 copy-start.36
  115.3 25.2 %copy-start.4 = (f32[985,384]{1,0:T(8,128)}, f32[985,384]{1,0:T(8,128)S(1)}, u32[]{:S(2)}) copy-start(f32[985,384]{1,0:T(8,128)S(1)} %get-tuple-element.75) | copy-start | bytes 4538884
  115.7 15.7 %copy-start.19 = (bf16[985,384]{1,0:T(8,128)(2,1)S(1)}, bf16[985,384]{1,0:T(8,128)(2,1)}, u32[]{:S(2)}) copy-start(bf16[985,384]{1,0:T(8,128)(2,1)} %param.17) | copy-start | bytes 2269444
  115.7 15.7 %copy-start.23 = (bf16[1536,384]{1,0:T(8,128)(2,1)S(1)}, bf16[1536,384]{1,0:T(8,128)(2,1)}, u32[]{:S(2)}) copy-start(bf16[1536,384]{1,0:T(8,128)(2,1)} %reshape.253) | copy-start | bytes 3538948
  141.2 1.7 copy-start.6
  146.1 9.2 %slice-start = ((s8[6144000]{0:T(1024)(128)(4,1)}), s8[1949696]{0:T(1024)(128)(4,1)S(1)}, s32[]{:S(2)}) async-start(s8[6144000]{0:T(1024)(128)(4,1)} %bitcast.229), calls=%async_computation.6 | async-start | bytes 3899392
  149.9 5.4 slice-start.1
  149.9 5.4 copy-start.15
  149.9 5.4 copy-start.16
  157.4 2.1 copy-start.11
  159.5 2.1 copy-start.13
  161.6 1.7 copy-start.20
  161.6 2.5 copy-start.37
  181.7 7.6 %copy-start.35 = (f32[384]{0:T(512)S(1)}, f32[384]{0:T(512)}, u32[]{:S(2)}) copy-start(f32[384]{0:T(512)} %get-tuple-element.70) | copy-start | bytes 4612
  205.0 118.2 %copy-start.25 = (f32[432,128]{1,0:T(8,128)S(1)}, f32[432,128]{1,0:T(8,128)}, u32[]{:S(2)}) copy-start(f32[432,128]{1,0:T(8,128)} %param.18) | copy-start | bytes 663556
  205.1 193.8 %all-gather.5.cloned.1.call-start = ((), (), s32[]{:S(2)}) async-start(), calls=%async_computation.4 | async-start | bytes 7299072 | tf_op jit(solution)/shard_map/all_gather | solution.py:197
  324.9 409.7 %reduce-scatter.5.cloned.1.call-start = ((), (), s32[]{:S(2)}) async-start(), calls=%async_computation.5 | async-start | bytes 7299072 | tf_op jit(solution)/shard_map/reduce_scatter | solution.py:208
  424.0 0.8 copy-start.22
  475.0 1.2 copy-start.17
  503.0 10.4 %copy-start.1 = (f32[384,1536]{1,0:T(8,128)S(1)}, f32[384,1536]{1,0:T(8,128)}, u32[]{:S(2)}) copy-start(f32[384,1536]{1,0:T(8,128)} %fusion.98) | copy-start | bytes 7077892 | tf_op jit(solution)/shard_map/cond
  503.0 10.4 %copy-start.2 = (f32[1536,384]{0,1:T(8,128)S(1)}, f32[1536,384]{0,1:T(8,128)}, u32[]{:S(2)}) copy-start(f32[1536,384]{0,1:T(8,128)} %copy.25) | copy-start | bytes 7077892 | tf_op jit(solution)/shard_map/cond
  536.8 6.1 copy-start.9
  552.3 1.4 copy-start.8
  619.5 1.8 copy-start.18
  621.2 3.0 copy-start.28
  624.2 1.4 copy-start.7
  624.2 1.7 copy-start.21
  625.9 38.9 %copy-start.29 = (f32[36,128]{1,0:T(8,128)S(1)}, f32[36,128]{1,0:T(8,128)}, u32[]{:S(2)}) copy-start(f32[36,128]{1,0:T(8,128)} %param.19) | copy-start | bytes 55300
  625.9 39.5 %copy-start.5 = (f32[985,384]{1,0:T(8,128)S(1)}, f32[985,384]{1,0:T(8,128)}, u32[]{:S(2)}) copy-start(f32[985,384]{1,0:T(8,128)} %copy-done.4) | copy-start | bytes 4538884
  625.9 39.5 %copy-start.33 = (f32[384]{0:T(512)S(1)}, f32[384]{0:T(512)}, u32[]{:S(2)}) copy-start(f32[384]{0:T(512)} %get-tuple-element.64) | copy-start | bytes 4612
  664.8 6.3 copy-start.26
Sparse Core Ops, SparseCore 0:
  10.9 62.7 all-gather.2
  205.2 118.0 reduce-scatter.2
  327.2 71.6 all-gather.4
  619.6 114.9 reduce-scatter.4
where the time goes:
time: 752 us; the launch traced here: 743 us
  waiting for transfers between devices  315 us (42%)
  matrix products  223 us (30%)
  local copies, waits for them, and re-layouts  93.4 us (12%)
  other arithmetic  54.2 us (7%)
  blocking collectives  37 us (5%)
  between operations  14.8 us (2%)
    reduce_scatter x1, waiting for transfers between devices, on_device(): lax.psum_scatter(local_grads, 'dp', scatter_dimension=0, tiled=True)  118 us
    all_gather x1, waiting for transfers between devices, on_device(): gathered = lax.all_gather(new_mom_weights, 'dp', axis=0, tiled=True)  73.9 us
    dot_general x20, matrix products, orthogonalize(): square = jnp.dot(current, current.T, precision=HIGH)  69.5 us
    dot_general x20, matrix products, orthogonalize(): current = first * current + jnp.dot(poly, current, precision=HIGH)  66.7 us
    reduce_scatter x1, waiting for transfers between devices, on_device(): lax.psum_scatter(owned_flat, 'dp', scatter_dimension=0, tiled=True)  63.5 us
    all_gather x1, waiting for transfers between devices, on_device(): whole = lax.all_gather(weights, 'dp', axis=0, tiled=True)  58.9 us
    psum x1, blocking collectives, on_device(): grad_vectors = lax.psum(local_vector_grads, 'dp')  37 us
    dot_general x20, matrix products, orthogonalize(): poly = second * square + third * jnp.dot(square, square, precision=HIGH)  26.1 us
  transfers between devices with their start and end apart: 4, of which 4 were waited for; matrix products, arithmetic and copies ran while one was open for 2% of the time, Pallas kernels for 0%

commit v1 on v0

--- a/solution.py
+++ b/solution.py
@@ -191,7 +191,7 @@
             grad_bias_up,
         ]
     ).reshape(-1, 128)
-    grad_vectors = lax.psum(local_vector_grads, "dp")
+    grad_vectors = jnp.sum(lax.all_gather(local_vector_grads, "dp"), axis=0)
     grad_weights = lax.psum_scatter(local_grads, "dp", scatter_dimension=0, tiled=True)
     new_mom_weights = MOMENTUM * mom_weights + grad_weights
     gathered = lax.all_gather(new_mom_weights, "dp", axis=0, tiled=True)

time: 752 us -> 752 us (level)
    all_gather x0 -> x1, blocking collectives: none -> 38.1 us  [on_device(): grad_vectors = jnp.sum(lax.all_gather(local_vector_grads, 'dp'), axis=0)]
    psum x1 -> x0, blocking collectives: 37 us -> none  [on_device(): grad_vectors = lax.psum(local_vector_grads, 'dp')]
where the time goes in v1:
time: 752 us; the launch traced here: 743 us
  waiting for transfers between devices  314 us (42%)
  matrix products  222 us (30%)
  local copies, waits for them, and re-layouts  93.4 us (12%)
  other arithmetic  54.3 us (7%)
  blocking collectives  38.1 us (5%)
  between operations  14.8 us (2%)
    reduce_scatter x1, waiting for transfers between devices, on_device(): lax.psum_scatter(local_grads, 'dp', scatter_dimension=0, tiled=True)  118 us
    all_gather x1, waiting for transfers between devices, on_device(): gathered = lax.all_gather(new_mom_weights, 'dp', axis=0, tiled=True)  73.9 us
    dot_general x20, matrix products, orthogonalize(): square = jnp.dot(current, current.T, precision=HIGH)  69.5 us
    dot_general x20, matrix products, orthogonalize(): current = first * current + jnp.dot(poly, current, precision=HIGH)  66.7 us
    reduce_scatter x1, waiting for transfers between devices, on_device(): lax.psum_scatter(owned_flat, 'dp', scatter_dimension=0, tiled=True)  62.8 us
    all_gather x1, waiting for transfers between devices, on_device(): whole = lax.all_gather(weights, 'dp', axis=0, tiled=True)  58.9 us
    all_gather x1, blocking collectives, on_device(): grad_vectors = jnp.sum(lax.all_gather(local_vector_grads, 'dp'), axis=0)  38.1 us
    dot_general x20, matrix products, orthogonalize(): poly = second * square + third * jnp.dot(square, square, precision=HIGH)  26.1 us
  transfers between devices with their start and end apart: 4, of which 4 were waited for; matrix products, arithmetic and copies ran while one was open for 2% of the time, Pallas kernels for 0%

profile of v1, /device:TPU:0, one launch (start us, length us, event | category | flops | bytes accessed | tf_op | source)
XLA Modules:
  0.0 743.2 jit_solution(17653688732029494299)
XLA Ops:
  14.8 58.9 %all-gather.3.cloned.1.call-done = bf16[13824,128]{1,0:T(8,128)(2,1)} async-done(((bf16[432,128]{1,0:T(8,128)(2,1)}), bf16[13824,128]{1,0:T(8,128)(2,1)}) %all-gather.3.cloned.1.call-update) | async-done | bytes 3538960 | tf_op jit(solution)/shard_map/all_gather | solution.py:92
  85.0 5.7 reshape.258
  90.7 5.8 fusion.79
  96.5 3.3 copy.68
  99.8 4.1 copy.67
  103.9 3.6 copy.69
  115.7 15.7 %multiply_convert_fusion.1 = (bf16[985,1536]{1,0:T(8,128)(2,1)}, f32[985,1536]{1,0:T(8,128)S(1)}, f32[985,1536]{1,0:T(8,128)S(1)}) fusion(f32[1536]{0:T(1024)S(1)} %copy-done.31, bf16[384,1536]{1,0:T(8,128)(2,1)S(1)} %copy-done.24, f32[985,384]{1,0:T(8,128)S(1)} %get-tuple-element.75, f32[384]{0:T(512)S(1)} %copy-done.36, f32[384]{0:T(512)S(1)} %get-tuple-element.66, ...), kind=kOutput, calls=%fused_computation.96 | convolution fusion | flops 1263699840 | bytes 17839304 | tf_op jit(solution)/shard_map/dot_general | solution.py:54
  131.5 4.0 convert_reduce_fusion
  146.1 3.8 copy.52
  149.9 5.4 convolution_bitcast_fusion
  164.0 3.3 fusion.102
  177.2 4.5 copy.57
  181.7 7.6 %convert_element_type.97 = bf16[985,1152]{0,1:T(8,128)(2,1)} reshape(bf16[5,197,3,6,64]{1,0,4,3,2:T(8,128)(2,1)} %copy.57) | data formatting | bytes 4538880 | tf_op jit(solution)/shard_map/convert_element_type | solution.py:168
  189.2 4.5 fusion.69
  196.2 8.8 %maximum_bitcast_fusion = f32[13824,128]{1,0:T(8,128)} fusion(f32[589824]{0:T(1024)S(1)} %reshape.255, f32[589824]{0:T(1024)} %reshape.254, f32[147456]{0:T(1024)} %reshape.253, f32[442368]{0:T(1024)} %reshape.252), kind=kLoop, calls=%fused_computation.87 | loop fusion | flops 5308416 | bytes 14155776 | tf_op jit(solution)/shard_map/reshape | solution.py:180
  205.1 118.2 %reduce-scatter.3.cloned.1.call-done = f32[432,128]{1,0:T(8,128)} async-done(((f32[13824,128]{1,0:T(8,128)}), f32[432,128]{1,0:T(8,128)}) %reduce-scatter.3.cloned.1.call-update) | async-done | bytes 221200 | tf_op jit(solution)/shard_map/reduce_scatter | solution.py:195
  325.0 73.9 %all-gather.5.cloned.1.call-done = f32[13824,128]{1,0:T(8,128)} async-done(((f32[432,128]{1,0:T(8,128)}), f32[13824,128]{1,0:T(8,128)}) %all-gather.5.cloned.1.call-update) | async-done | bytes 7077904 | tf_op jit(solution)/shard_map/all_gather | solution.py:197
  398.9 25.2 %conditional.5 = (f32[147456]{0:T(1024)S(1)}) conditional(s32[]{:T(128)} %convert_element_type.102, () %tuple.41, f32[13824,128]{1,0:T(8,128)} %all-gather.5.cloned.1.call-done), branch_computations={%region_25.0_spmd, %region_26.28_spmd} | conditional | flops 10196287488 | bytes 24772644 | solution.py:203
  424.9 50.1 %conditional.4 = (f32[442368]{0:T(1024)S(1)}) conditional(s32[]{:T(128)} %convert_element_type.102, () %tuple.40, f32[13824,128]{1,0:T(8,128)} %all-gather.5.cloned.1.call-done), branch_computations={%region_22.0_spmd, %region_23.25_spmd} | conditional | flops 23789666304 | bytes 50724900 | solution.py:203
  456.1 3.4 fusion.85
  468.6 4.5 convolution_add_fusion
  476.2 76.1 %conditional.7 = (f32[589824]{0:T(1024)S(1)}) conditional(s32[]{:T(128)} %convert_element_type.102, () %tuple.43, f32[13824,128]{1,0:T(8,128)} %all-gather.5.cloned.1.call-done), branch_computations={%region_31.32_spmd, %region_32.34_spmd} | conditional | flops 30598152192 | bytes 141557856 | solution.py:203
  479.8 3.4 broadcast_multiply_fusion
  490.5 3.9 fusion.97
  495.7 5.3 fusion.98
  503.0 9.1 %fusion.32 = f32[384,384]{1,0:T(8,128)S(1)} fusion(f32[384,1536]{1,0:T(8,128)} %fusion.98, f32[1536,384]{0,1:T(8,128)} %copy.42), kind=kOutput, calls=%fused_computation.85 | convolution fusion | flops 2719088640 | bytes 5308416 | tf_op jit(solution)/shard_map/cond/branch_1_fun/dot_general | solution.py:79
  513.4 4.3 multiply_add_fusion.2
  517.7 4.0 fusion.99
  523.0 4.3 fusion.100
  527.3 4.2 fusion.30
  532.8 4.0 fusion.29
  536.8 4.7 fusion.19
  542.8 4.9 convolution_add_fusion.15
  553.7 58.4 %conditional.6 = (f32[589824]{0:T(1024)}) conditional(s32[]{:T(128)} %convert_element_type.102, () %tuple.42, f32[13824,128]{1,0:T(8,128)} %all-gather.5.cloned.1.call-done), branch_computations={%region_28.0_spmd, %region_29.31_spmd} | conditional | flops 30586355712 | bytes 63701028 | solution.py:203
  562.9 4.0 fusion.92
  568.2 4.0 convolution_add_fusion.14
  572.2 4.5 fusion.93
  578.0 4.0 convolution_add_fusion.13
  582.0 4.0 fusion.94
  587.3 4.2 convolution_add_fusion.12
  591.5 4.0 fusion.95
  596.8 4.0 convolution_add_fusion.11
  600.8 4.2 fusion.96
  606.4 4.0 convolution_add_fusion.10
  612.2 7.3 maximum_bitcast_fusion.1
  627.8 38.1 %all_gather.15 = f32[32,36,128]{2,1,0:T(8,128)S(1)} all-gather(f32[1,36,128]{2,1,0:T(8,128)S(1)} %bitcast.231), channel_id=1, replica_groups=mesh['dp'=32] {'dp'}, dimensions={0}, use_global_device_ids=true | all-gather | bytes 608256 | tf_op jit(solution)/shard_map/all_gather | solution.py:194
  666.5 5.2 add_convert_fusion.1
  671.8 62.8 %reduce-scatter.5.cloned.1.call-done = f32[432,128]{1,0:T(8,128)} async-done(((f32[13824,128]{1,0:T(8,128)}), f32[432,128]{1,0:T(8,128)}) %reduce-scatter.5.cloned.1.call-update) | async-done | bytes 221200 | tf_op jit(solution)/shard_map/reduce_scatter | solution.py:208
  (211 shorter events, 177.4 us)
Async XLA Ops:
  7.2 66.5 %all-gather.3.cloned.1.call-start = ((), (), s32[]{:S(2)}) async-start(), calls=%async_computation.2 | async-start | bytes 3649536 | tf_op jit(solution)/shard_map/all_gather | solution.py:92
  7.9 315.4 %reduce-scatter.3.cloned.1.call-start = ((), (), s32[]{:S(2)}) async-start(), calls=%async_computation.3 | async-start | bytes 7299072 | tf_op jit(solution)/shard_map/reduce_scatter | solution.py:195
  12.9 0.6 copy-start.27
  73.7 1.3 slice-start.2
  78.7 3.6 copy-start.3
  78.7 3.6 copy-start.30
  78.7 3.6 copy-start.34
  99.8 7.6 %copy-start.10 = (bf16[5,197,1,6,64]{1,4,3,0,2:T(8,128)(2,1)}, bf16[5,197,1,6,64]{1,4,3,0,2:T(8,128)(2,1)S(1)}, u32[]{:S(2)}) copy-start(bf16[5,197,1,6,64]{1,4,3,0,2:T(8,128)(2,1)S(1)} %copy.68) | copy-start | bytes 2269444
  107.5 1.1 copy-start.12
  108.5 2.6 copy-start
  108.6 2.6 copy-start.14
  112.4 2.0 copy-start.32
  114.4 1.3 copy-start.24
  114.4 1.3 copy-start.31
  114.5 1.3 copy-start.36
  115.3 25.2 %copy-start.4 = (f32[985,384]{1,0:T(8,128)}, f32[985,384]{1,0:T(8,128)S(1)}, u32[]{:S(2)}) copy-start(f32[985,384]{1,0:T(8,128)S(1)} %get-tuple-element.75) | copy-start | bytes 4538884
  115.7 15.7 %copy-start.19 = (bf16[985,384]{1,0:T(8,128)(2,1)S(1)}, bf16[985,384]{1,0:T(8,128)(2,1)}, u32[]{:S(2)}) copy-start(bf16[985,384]{1,0:T(8,128)(2,1)} %param.17) | copy-start | bytes 2269444
  115.7 15.7 %copy-start.23 = (bf16[1536,384]{1,0:T(8,128)(2,1)S(1)}, bf16[1536,384]{1,0:T(8,128)(2,1)}, u32[]{:S(2)}) copy-start(bf16[1536,384]{1,0:T(8,128)(2,1)} %reshape.250) | copy-start | bytes 3538948
  141.2 1.7 copy-start.6
  146.1 9.2 %slice-start = ((s8[6144000]{0:T(1024)(128)(4,1)}), s8[1949696]{0:T(1024)(128)(4,1)S(1)}, s32[]{:S(2)}) async-start(s8[6144000]{0:T(1024)(128)(4,1)} %bitcast.229), calls=%async_computation.6 | async-start | bytes 3899392
  149.9 5.4 slice-start.1
  149.9 5.4 copy-start.15
  149.9 5.4 copy-start.16
  157.4 2.1 copy-start.11
  159.5 2.1 copy-start.13
  161.6 1.7 copy-start.20
  161.6 2.5 copy-start.37
  181.7 7.6 %copy-start.35 = (f32[384]{0:T(512)S(1)}, f32[384]{0:T(512)}, u32[]{:S(2)}) copy-start(f32[384]{0:T(512)} %get-tuple-element.70) | copy-start | bytes 4612
  205.0 118.2 %copy-start.25 = (f32[432,128]{1,0:T(8,128)S(1)}, f32[432,128]{1,0:T(8,128)}, u32[]{:S(2)}) copy-start(f32[432,128]{1,0:T(8,128)} %param.18) | copy-start | bytes 663556
  205.1 193.8 %all-gather.5.cloned.1.call-start = ((), (), s32[]{:S(2)}) async-start(), calls=%async_computation.4 | async-start | bytes 7299072 | tf_op jit(solution)/shard_map/all_gather | solution.py:197
  324.9 409.6 %reduce-scatter.5.cloned.1.call-start = ((), (), s32[]{:S(2)}) async-start(), calls=%async_computation.5 | async-start | bytes 7299072 | tf_op jit(solution)/shard_map/reduce_scatter | solution.py:208
  424.0 0.8 copy-start.22
  475.0 1.2 copy-start.17
  503.0 10.4 %copy-start.1 = (f32[384,1536]{1,0:T(8,128)S(1)}, f32[384,1536]{1,0:T(8,128)}, u32[]{:S(2)}) copy-start(f32[384,1536]{1,0:T(8,128)} %fusion.98) | copy-start | bytes 7077892 | tf_op jit(solution)/shard_map/cond
  503.0 10.4 %copy-start.2 = (f32[1536,384]{0,1:T(8,128)S(1)}, f32[1536,384]{0,1:T(8,128)}, u32[]{:S(2)}) copy-start(f32[1536,384]{0,1:T(8,128)} %copy.42) | copy-start | bytes 7077892 | tf_op jit(solution)/shard_map/cond
  536.8 6.1 copy-start.9
  552.3 1.4 copy-start.8
  619.5 1.8 copy-start.18
  621.2 3.0 copy-start.28
  624.2 1.5 copy-start.7
  624.2 1.7 copy-start.21
  625.9 40.0 %copy-start.29 = (f32[36,128]{1,0:T(8,128)S(1)}, f32[36,128]{1,0:T(8,128)}, u32[]{:S(2)}) copy-start(f32[36,128]{1,0:T(8,128)} %param.19) | copy-start | bytes 55300
  625.9 40.6 %copy-start.5 = (f32[985,384]{1,0:T(8,128)S(1)}, f32[985,384]{1,0:T(8,128)}, u32[]{:S(2)}) copy-start(f32[985,384]{1,0:T(8,128)} %copy-done.4) | copy-start | bytes 4538884
  625.9 40.6 %copy-start.33 = (f32[384]{0:T(512)S(1)}, f32[384]{0:T(512)}, u32[]{:S(2)}) copy-start(f32[384]{0:T(512)} %get-tuple-element.64) | copy-start | bytes 4612
  665.9 5.9 copy-start.26
Sparse Core Ops, SparseCore 0:
  10.9 62.7 all-gather.2
  205.2 118.0 reduce-scatter.2
  327.2 71.6 all-gather.4
  619.6 114.9 reduce-scatter.4
